TPU v7x, 512 devices: a whole 4x4x16 slice. The times are simulated.
512 devices in a mesh: ctx: 64 (over x, y, z_lo), head: 8 (over z_hi, core).
Axes of the slice: x: 4, y: 4, z: 16 (z_hi: 4, z_lo: 4; z = z_hi * 4 + z_lo), core: 2. Of those that a mesh axis runs over, the one named last changes fastest.
Arguments:
- hidden: bfloat16 [8192, 7168], P('ctx', 'head'), may hold values from -6 to 6
- w_dkv: bfloat16 [7168, 576], P('head'), may hold values from -0.0625 to 0.0625
- kv_gain: float32 [512], replicated, may hold values from 0.25 to 1.75
- w_uk: bfloat16 [512, 6144], P(None, 'head'), may hold values from -0.25 to 0.25
- w_uv: bfloat16 [512, 6144], P(None, 'head'), may hold values from -0.25 to 0.25
- queries: bfloat16 [8192, 9216], P('ctx', 'head'), may hold values from -140 to 140
- segments: int32 [8192], P('ctx'), may hold values from 0 to 2, as said below
- positions: int32 [8192], P('ctx'), may hold values from 0 to 6143, as said below
Outputs:
- attended: bfloat16 [8192, 6144], P('ctx', 'head')
Inputs may be any that keep to these rules, and one draw needn't show every extreme that they name: `segments`: 0 marks the shared video prompt, 1 the chosen caption, 2 the rejected caption; ids never fall along the sequence; the prompt holds 2048 to 4096 tokens, one of the two captions exactly 2048 tokens and the other the rest. `positions`: a token's index in the sequence for the prompt and the chosen caption; for the rejected caption its index minus the chosen caption's length, so that it continues the prompt.
All inputs are finite; a program needn't handle non-finite values.
Results may differ from a plain program's by a relative error of at most 0.012.
The roundings to bfloat16 on the way count: a program that leaves them out, or rounds other values in their place, can miss the bound.
Values may be sent and summed in bfloat16 or wider, within the bound.
A program may use at most 64 MiB of HBM per device.

v0:
```python
import math

import jax
import jax.numpy as jnp
from jax import lax
from jax.sharding import PartitionSpec as P

KVL = 512
RD = 64
NOPE = 128
VD = 128


ROPE_BASE = 10000.0
NORM_EPS = 1e-06


def rotary(values, positions):
    half_width = values.shape[-1] // 2
    frequency = jnp.exp(
        jnp.arange(half_width, dtype=jnp.float32) * (-2.0 * math.log(ROPE_BASE) / values.shape[-1])
    )
    angles = positions.astype(jnp.float32)[..., None] * frequency
    cosine = jnp.cos(angles)
    sine_part = jnp.sin(angles)
    first_half = values[..., :half_width]
    second = values[..., half_width:]
    return jnp.concatenate(
        [first_half * cosine - second * sine_part, second * cosine + first_half * sine_part],
        axis=-1,
    )


def finish_keys(latent, positions, kv_gain):
    compressed = latent[:, :KVL]
    mean_square = jnp.mean(compressed * compressed, axis=-1, keepdims=True)
    normed = (compressed * lax.rsqrt(mean_square + NORM_EPS) * kv_gain).astype(jnp.bfloat16)
    rope_part = rotary(latent[:, KVL:], positions).astype(jnp.bfloat16)
    return jnp.concatenate([normed, rope_part], axis=-1)


def shards(hidden, w_dkv, kv_gain, w_uk, w_uv, queries, segments, positions):
    row_count = hidden.shape[0]
    head_count = w_uk.shape[1] // NOPE
    score_scale = 1.0 / math.sqrt(NOPE + RD)
    first_row = lax.axis_index("ctx") * row_count
    query_index = first_row + jnp.arange(row_count, dtype=jnp.int32)
    last_query = first_row + (row_count - 1)
    shaped = queries.reshape(row_count, head_count, NOPE + RD)
    query_rope = rotary(shaped[:, :, NOPE:].astype(jnp.float32), positions[:, None]).astype(
        jnp.bfloat16
    )
    absorbed = jnp.einsum(
        "rhn,khn->rhk",
        shaped[:, :, :NOPE],
        w_uk.reshape(KVL, head_count, NOPE),
        preferred_element_type=jnp.float32,
    ).astype(jnp.bfloat16)
    query_full = jnp.concatenate([absorbed, query_rope], axis=-1).reshape(
        row_count * head_count, KVL + RD
    )

    def attend(softmax_state, key_block, segment_block, block_start):
        key_count = key_block.shape[0]
        key_index = block_start + jnp.arange(key_count, dtype=jnp.int32)
        visible = (key_index[None, :] <= query_index[:, None]) & (
            (segment_block[None, :] == segments[:, None]) | (segment_block[None, :] == 0)
        )

        def compute(running):
            top_score, weight_sum, mixture = running
            scores = (
                lax.dot_general(
                    query_full,
                    key_block,
                    (((1,), (1,)), ((), ())),
                    preferred_element_type=jnp.float32,
                ).reshape(row_count, head_count, key_count)
                * score_scale
            )
            visible_mask = visible[:, None, :]
            new_top = jnp.maximum(
                top_score, jnp.max(jnp.where(visible_mask, scores, -1e30), axis=-1)
            )
            weights = jnp.where(visible_mask, jnp.exp(scores - new_top[..., None]), 0.0)
            shrink = jnp.exp(top_score - new_top)
            weight_sum = weight_sum * shrink + jnp.sum(weights, axis=-1)
            update = jnp.dot(
                weights.astype(jnp.bfloat16).reshape(row_count * head_count, key_count),
                key_block[:, :KVL],
                preferred_element_type=jnp.float32,
            ).reshape(row_count, head_count, KVL)
            mixture = mixture * shrink[..., None] + update
            return (new_top, weight_sum, mixture)

        active = block_start <= last_query
        return lax.cond(active, compute, lambda unchanged: unchanged, softmax_state)

    initial = (
        jnp.full((row_count, head_count), -1e30, jnp.float32),
        jnp.zeros((row_count, head_count), jnp.float32),
        jnp.zeros((row_count, head_count, KVL), jnp.float32),
    )
    latent = lax.psum(jnp.dot(hidden, w_dkv, preferred_element_type=jnp.float32), "head")
    key_rows = finish_keys(latent, positions, kv_gain)
    absorb_key_rows = lax.all_gather(key_rows, "ctx", axis=0, tiled=True)
    key_segments = lax.all_gather(segments, "ctx", axis=0, tiled=True)
    key_count = absorb_key_rows.shape[0]
    block_total = key_count // 512
    block_starts = 512 * jnp.arange(block_total, dtype=jnp.int32)

    def advance(running, members):
        return (attend(running, members[0], members[1], members[2]), None)

    final_state = lax.scan(
        advance,
        initial,
        (
            absorb_key_rows.reshape(block_total, 512, KVL + RD),
            key_segments.reshape(block_total, 512),
            block_starts,
        ),
    )[0]
    weight_sum = final_state[1]
    mixed_latent = (final_state[2] / weight_sum[..., None]).astype(jnp.bfloat16)
    attended = jnp.einsum(
        "rhk,khv->rhv",
        mixed_latent,
        w_uv.reshape(KVL, head_count, VD),
        preferred_element_type=jnp.float32,
    ).astype(jnp.bfloat16)
    return attended.reshape(row_count, head_count * VD)


def solution(mesh):
    in_specs = (
        P("ctx", "head"),
        P("head", None),
        P(),
        P(None, "head"),
        P(None, "head"),
        P("ctx", "head"),
        P("ctx"),
        P("ctx"),
    )
    out_specs = P("ctx", "head")
    return jax.shard_map(shards, mesh=mesh, in_specs=in_specs, out_specs=out_specs, check_vma=False)
```

profile of v0, /device:TPU:94, one launch (start us, length us, event | category | flops | bytes accessed | tf_op | source)
XLA Modules:
  0.0 724.8 jit_solution(2783626783076373457)
XLA Ops:
  7.8 2.1 fusion.10
  9.9 99.8 %all-reduce.2.cloned.1.call-done = f32[128,576]{0,1:T(8,128)} async-done(((f32[128,576]{0,1:T(8,128)}), f32[128,576]{0,1:T(8,128)}) %all-reduce.2.cloned.1.call-update) | async-done | bytes 294928 | tf_op jit(solution)/shard_map/psum | solution.py:104
  114.1 173.8 %all-gather = s32[64,1,128]{2,1,0:T(1,128)S(1)} all-gather(s32[1,1,128]{2,1,0:T(1,128)S(1)} %bitcast.47), channel_id=1, replica_groups=mesh['ctx'=64,'head'=8] {'ctx'}, dimensions={0}, use_global_device_ids=true | all-gather | bytes 33280 | tf_op jit(solution)/shard_map/all_gather | solution.py:107
  289.6 2.3 copy.44
  295.2 179.4 %all-gather.3.cloned.1.call-done = bf16[8192,576]{0,1:T(8,128)(2,1)} async-done(((bf16[128,576]{0,1:T(8,128)(2,1)}), bf16[8192,576]{0,1:T(8,128)(2,1)}) %all-gather.3.cloned.1.call-update) | async-done | bytes 9437200 | tf_op jit(solution)/shard_map/all_gather | solution.py:106
  474.6 14.1 %copy.47 = bf16[8192,576]{1,0:T(8,128)(2,1)} copy(bf16[8192,576]{0,1:T(8,128)(2,1)} %all-gather.3.cloned.1.call-done) | data formatting | bytes 18874368
  490.1 224.9 %while.15 = (s32[]{:T(128)}, f32[128,6]{1,0:T(8,128)S(1)}, f32[128,6]{1,0:T(8,128)S(1)}, f32[128,6,512]{2,0,1:T(8,128)}, s32[16]{0:T(128)S(1)}, /*index=5*/s32[]...) while((s32[]{:T(128)}, f32[128,6]{1,0:T(8,128)S(1)}, ...), condition=%wide.region_7.8_spmd.clone, body=%wide.region_2.7_spmd.clone.sunk | while | flops 859441792 | bytes 21012420 | solution.py:115
  491.4 12.7 %conditional.3 = ((f32[128,6]{1,0:T(8,128)S(1)}, f32[128,6]{1,0:T(8,128)S(1)}, f32[128,6,512]{2,0,1:T(8,128)})) conditional(s32[]{:T(128)} %convert_element_type.57, (f32[128,6]{1,0:T(8,128)S(1)}, f32[128,6]{1,0:T(8,128)S(1)}, f32[128,6,512]{2,0,1:T(8,128)}) %tuple.51, (s32[]{:T(128)}, s32[1,512]{1,0:T(1,128)S(1)}, s32[]{:T(128)}, ...), branch_computations={%region_3.3_spmd, %region_4.6_spmd} | conditional | flops 859441792 | bytes 21009596 | solution.py:97
  500.9 3.2 multiply_add_fusion
  505.5 12.7 %conditional.3 = ((f32[128,6]{1,0:T(8,128)S(1)}, f32[128,6]{1,0:T(8,128)S(1)}, f32[128,6,512]{2,0,1:T(8,128)})) conditional(s32[]{:T(128)} %convert_element_type.57, (f32[128,6]{1,0:T(8,128)S(1)}, f32[128,6]{1,0:T(8,128)S(1)}, f32[128,6,512]{2,0,1:T(8,128)}) %tuple.51, (s32[]{:T(128)}, s32[1,512]{1,0:T(1,128)S(1)}, s32[]{:T(128)}, ...), branch_computations={%region_3.3_spmd, %region_4.6_spmd} | conditional | flops 859441792 | bytes 21009596 | solution.py:97
  509.3 2.1 fusion.2
  514.9 3.2 multiply_add_fusion
  519.6 12.7 %conditional.3 = ((f32[128,6]{1,0:T(8,128)S(1)}, f32[128,6]{1,0:T(8,128)S(1)}, f32[128,6,512]{2,0,1:T(8,128)})) conditional(s32[]{:T(128)} %convert_element_type.57, (f32[128,6]{1,0:T(8,128)S(1)}, f32[128,6]{1,0:T(8,128)S(1)}, f32[128,6,512]{2,0,1:T(8,128)}) %tuple.51, (s32[]{:T(128)}, s32[1,512]{1,0:T(1,128)S(1)}, s32[]{:T(128)}, ...), branch_computations={%region_3.3_spmd, %region_4.6_spmd} | conditional | flops 859441792 | bytes 21009596 | solution.py:97
  523.4 2.1 fusion.2
  529.0 3.2 multiply_add_fusion
  533.6 12.7 %conditional.3 = ((f32[128,6]{1,0:T(8,128)S(1)}, f32[128,6]{1,0:T(8,128)S(1)}, f32[128,6,512]{2,0,1:T(8,128)})) conditional(s32[]{:T(128)} %convert_element_type.57, (f32[128,6]{1,0:T(8,128)S(1)}, f32[128,6]{1,0:T(8,128)S(1)}, f32[128,6,512]{2,0,1:T(8,128)}) %tuple.51, (s32[]{:T(128)}, s32[1,512]{1,0:T(1,128)S(1)}, s32[]{:T(128)}, ...), branch_computations={%region_3.3_spmd, %region_4.6_spmd} | conditional | flops 859441792 | bytes 21009596 | solution.py:97
  537.5 2.1 fusion.2
  543.0 3.2 multiply_add_fusion
  547.7 12.7 %conditional.3 = ((f32[128,6]{1,0:T(8,128)S(1)}, f32[128,6]{1,0:T(8,128)S(1)}, f32[128,6,512]{2,0,1:T(8,128)})) conditional(s32[]{:T(128)} %convert_element_type.57, (f32[128,6]{1,0:T(8,128)S(1)}, f32[128,6]{1,0:T(8,128)S(1)}, f32[128,6,512]{2,0,1:T(8,128)}) %tuple.51, (s32[]{:T(128)}, s32[1,512]{1,0:T(1,128)S(1)}, s32[]{:T(128)}, ...), branch_computations={%region_3.3_spmd, %region_4.6_spmd} | conditional | flops 859441792 | bytes 21009596 | solution.py:97
  551.5 2.1 fusion.2
  557.1 3.2 multiply_add_fusion
  561.7 12.7 %conditional.3 = ((f32[128,6]{1,0:T(8,128)S(1)}, f32[128,6]{1,0:T(8,128)S(1)}, f32[128,6,512]{2,0,1:T(8,128)})) conditional(s32[]{:T(128)} %convert_element_type.57, (f32[128,6]{1,0:T(8,128)S(1)}, f32[128,6]{1,0:T(8,128)S(1)}, f32[128,6,512]{2,0,1:T(8,128)}) %tuple.51, (s32[]{:T(128)}, s32[1,512]{1,0:T(1,128)S(1)}, s32[]{:T(128)}, ...), branch_computations={%region_3.3_spmd, %region_4.6_spmd} | conditional | flops 859441792 | bytes 21009596 | solution.py:97
  565.6 2.1 fusion.2
  571.1 3.2 multiply_add_fusion
  575.8 12.7 %conditional.3 = ((f32[128,6]{1,0:T(8,128)S(1)}, f32[128,6]{1,0:T(8,128)S(1)}, f32[128,6,512]{2,0,1:T(8,128)})) conditional(s32[]{:T(128)} %convert_element_type.57, (f32[128,6]{1,0:T(8,128)S(1)}, f32[128,6]{1,0:T(8,128)S(1)}, f32[128,6,512]{2,0,1:T(8,128)}) %tuple.51, (s32[]{:T(128)}, s32[1,512]{1,0:T(1,128)S(1)}, s32[]{:T(128)}, ...), branch_computations={%region_3.3_spmd, %region_4.6_spmd} | conditional | flops 859441792 | bytes 21009596 | solution.py:97
  579.6 2.1 fusion.2
  585.2 3.2 multiply_add_fusion
  589.8 12.7 %conditional.3 = ((f32[128,6]{1,0:T(8,128)S(1)}, f32[128,6]{1,0:T(8,128)S(1)}, f32[128,6,512]{2,0,1:T(8,128)})) conditional(s32[]{:T(128)} %convert_element_type.57, (f32[128,6]{1,0:T(8,128)S(1)}, f32[128,6]{1,0:T(8,128)S(1)}, f32[128,6,512]{2,0,1:T(8,128)}) %tuple.51, (s32[]{:T(128)}, s32[1,512]{1,0:T(1,128)S(1)}, s32[]{:T(128)}, ...), branch_computations={%region_3.3_spmd, %region_4.6_spmd} | conditional | flops 859441792 | bytes 21009596 | solution.py:97
  593.7 2.1 fusion.2
  599.2 3.2 multiply_add_fusion
  603.9 12.7 %conditional.3 = ((f32[128,6]{1,0:T(8,128)S(1)}, f32[128,6]{1,0:T(8,128)S(1)}, f32[128,6,512]{2,0,1:T(8,128)})) conditional(s32[]{:T(128)} %convert_element_type.57, (f32[128,6]{1,0:T(8,128)S(1)}, f32[128,6]{1,0:T(8,128)S(1)}, f32[128,6,512]{2,0,1:T(8,128)}) %tuple.51, (s32[]{:T(128)}, s32[1,512]{1,0:T(1,128)S(1)}, s32[]{:T(128)}, ...), branch_computations={%region_3.3_spmd, %region_4.6_spmd} | conditional | flops 859441792 | bytes 21009596 | solution.py:97
  607.7 2.1 fusion.2
  613.3 3.2 multiply_add_fusion
  617.9 12.7 %conditional.3 = ((f32[128,6]{1,0:T(8,128)S(1)}, f32[128,6]{1,0:T(8,128)S(1)}, f32[128,6,512]{2,0,1:T(8,128)})) conditional(s32[]{:T(128)} %convert_element_type.57, (f32[128,6]{1,0:T(8,128)S(1)}, f32[128,6]{1,0:T(8,128)S(1)}, f32[128,6,512]{2,0,1:T(8,128)}) %tuple.51, (s32[]{:T(128)}, s32[1,512]{1,0:T(1,128)S(1)}, s32[]{:T(128)}, ...), branch_computations={%region_3.3_spmd, %region_4.6_spmd} | conditional | flops 859441792 | bytes 21009596 | solution.py:97
  627.4 3.2 multiply_add_fusion
  632.0 12.7 %conditional.3 = ((f32[128,6]{1,0:T(8,128)S(1)}, f32[128,6]{1,0:T(8,128)S(1)}, f32[128,6,512]{2,0,1:T(8,128)})) conditional(s32[]{:T(128)} %convert_element_type.57, (f32[128,6]{1,0:T(8,128)S(1)}, f32[128,6]{1,0:T(8,128)S(1)}, f32[128,6,512]{2,0,1:T(8,128)}) %tuple.51, (s32[]{:T(128)}, s32[1,512]{1,0:T(1,128)S(1)}, s32[]{:T(128)}, ...), branch_computations={%region_3.3_spmd, %region_4.6_spmd} | conditional | flops 859441792 | bytes 21009596 | solution.py:97
  641.4 3.2 multiply_add_fusion
  646.0 12.7 %conditional.3 = ((f32[128,6]{1,0:T(8,128)S(1)}, f32[128,6]{1,0:T(8,128)S(1)}, f32[128,6,512]{2,0,1:T(8,128)})) conditional(s32[]{:T(128)} %convert_element_type.57, (f32[128,6]{1,0:T(8,128)S(1)}, f32[128,6]{1,0:T(8,128)S(1)}, f32[128,6,512]{2,0,1:T(8,128)}) %tuple.51, (s32[]{:T(128)}, s32[1,512]{1,0:T(1,128)S(1)}, s32[]{:T(128)}, ...), branch_computations={%region_3.3_spmd, %region_4.6_spmd} | conditional | flops 859441792 | bytes 21009596 | solution.py:97
  649.9 2.1 fusion.2
  655.5 3.2 multiply_add_fusion
  660.1 12.7 %conditional.3 = ((f32[128,6]{1,0:T(8,128)S(1)}, f32[128,6]{1,0:T(8,128)S(1)}, f32[128,6,512]{2,0,1:T(8,128)})) conditional(s32[]{:T(128)} %convert_element_type.57, (f32[128,6]{1,0:T(8,128)S(1)}, f32[128,6]{1,0:T(8,128)S(1)}, f32[128,6,512]{2,0,1:T(8,128)}) %tuple.51, (s32[]{:T(128)}, s32[1,512]{1,0:T(1,128)S(1)}, s32[]{:T(128)}, ...), branch_computations={%region_3.3_spmd, %region_4.6_spmd} | conditional | flops 859441792 | bytes 21009596 | solution.py:97
  669.5 3.2 multiply_add_fusion
  674.2 12.7 %conditional.3 = ((f32[128,6]{1,0:T(8,128)S(1)}, f32[128,6]{1,0:T(8,128)S(1)}, f32[128,6,512]{2,0,1:T(8,128)})) conditional(s32[]{:T(128)} %convert_element_type.57, (f32[128,6]{1,0:T(8,128)S(1)}, f32[128,6]{1,0:T(8,128)S(1)}, f32[128,6,512]{2,0,1:T(8,128)}) %tuple.51, (s32[]{:T(128)}, s32[1,512]{1,0:T(1,128)S(1)}, s32[]{:T(128)}, ...), branch_computations={%region_3.3_spmd, %region_4.6_spmd} | conditional | flops 859441792 | bytes 21009596 | solution.py:97
  683.6 3.2 multiply_add_fusion
  688.2 12.7 %conditional.3 = ((f32[128,6]{1,0:T(8,128)S(1)}, f32[128,6]{1,0:T(8,128)S(1)}, f32[128,6,512]{2,0,1:T(8,128)})) conditional(s32[]{:T(128)} %convert_element_type.57, (f32[128,6]{1,0:T(8,128)S(1)}, f32[128,6]{1,0:T(8,128)S(1)}, f32[128,6,512]{2,0,1:T(8,128)}) %tuple.51, (s32[]{:T(128)}, s32[1,512]{1,0:T(1,128)S(1)}, s32[]{:T(128)}, ...), branch_computations={%region_3.3_spmd, %region_4.6_spmd} | conditional | flops 859441792 | bytes 21009596 | solution.py:97
  697.6 3.2 multiply_add_fusion
  702.3 12.7 %conditional.3 = ((f32[128,6]{1,0:T(8,128)S(1)}, f32[128,6]{1,0:T(8,128)S(1)}, f32[128,6,512]{2,0,1:T(8,128)})) conditional(s32[]{:T(128)} %convert_element_type.57, (f32[128,6]{1,0:T(8,128)S(1)}, f32[128,6]{1,0:T(8,128)S(1)}, f32[128,6,512]{2,0,1:T(8,128)}) %tuple.51, (s32[]{:T(128)}, s32[1,512]{1,0:T(1,128)S(1)}, s32[]{:T(128)}, ...), branch_computations={%region_3.3_spmd, %region_4.6_spmd} | conditional | flops 859441792 | bytes 21009596 | solution.py:97
  711.7 3.2 multiply_add_fusion
  (544 shorter events, 155.1 us)
Async XLA Ops:
  6.5 3.4 copy-start.10
  6.5 105.2 %copy-start.9 = (f32[512]{0:T(512)S(1)}, f32[512]{0:T(512)}, u32[]{:S(2)}) copy-start(f32[512]{0:T(512)} %param.14) | copy-start | bytes 6148
  6.5 107.0 %copy-start.7 = (bf16[128,1152]{1,0:T(8,128)(2,1)S(1)}, bf16[128,1152]{1,0:T(8,128)(2,1)}, u32[]{:S(2)}) copy-start(bf16[128,1152]{1,0:T(8,128)(2,1)} %param.17) | copy-start | bytes 884740
  6.5 107.2 %copy-start.6 = (bf16[512,768]{1,0:T(8,128)(2,1)S(1)}, bf16[512,768]{1,0:T(8,128)(2,1)}, u32[]{:S(2)}) copy-start(bf16[512,768]{1,0:T(8,128)(2,1)} %param.15) | copy-start | bytes 2359300
  6.5 103.2 %all-reduce.2.cloned.1.call-start = ((), (), s32[]{:S(2)}) async-start(), calls=%async_computation | async-start | bytes 589824 | tf_op jit(solution)/shard_map/psum | solution.py:104
  9.9 464.8 %all-gather.3.cloned.1.call-start = ((), (), s32[]{:S(2)}) async-start(), calls=%async_computation.1 | async-start | bytes 9584640 | tf_op jit(solution)/shard_map/all_gather | solution.py:106
  110.8 3.2 copy-start.8
  497.5 2.1 copy-start.1
  500.8 3.2 copy-start.2
  500.9 3.2 copy-start.4
  511.6 2.1 copy-start.1
  514.9 3.2 copy-start.2
  514.9 3.2 copy-start.4
  525.6 2.1 copy-start.1
  529.0 3.2 copy-start.2
  529.0 3.2 copy-start.4
  539.7 2.1 copy-start.1
  543.0 3.2 copy-start.2
  543.0 3.2 copy-start.4
  553.7 2.1 copy-start.1
  557.1 3.2 copy-start.2
  557.1 3.2 copy-start.4
  567.8 2.1 copy-start.1
  571.1 3.2 copy-start.2
  571.1 3.2 copy-start.4
  581.9 2.1 copy-start.1
  585.2 3.2 copy-start.2
  585.2 3.2 copy-start.4
  595.9 2.1 copy-start.1
  599.2 3.2 copy-start.2
  599.2 3.2 copy-start.4
  610.0 2.1 copy-start.1
  613.3 3.2 copy-start.2
  613.3 3.2 copy-start.4
  627.3 3.2 copy-start.2
  627.3 3.2 copy-start.4
  641.4 3.2 copy-start.2
  641.4 3.2 copy-start.4
  655.4 3.2 copy-start.2
  655.5 3.2 copy-start.4
  669.5 3.2 copy-start.2
  669.5 3.2 copy-start.4
  683.6 3.2 copy-start.2
  683.6 3.2 copy-start.4
  697.6 3.2 copy-start.2
  697.6 3.2 copy-start.4
  711.7 3.2 copy-start.2
  711.7 3.2 copy-start.4
  (40 other events, 52.7 us)
Sparse Core Ops, SparseCore 0:
  10.3 99.4 all-reduce.1
  113.6 360.9 all-gather.2
where the time goes:
time: 728 us; the launch traced here: 725 us
  waiting for transfers between devices  279 us (38%)
  blocking collectives  174 us (24%)
  local copies, waits for them, and re-layouts  94.9 us (13%)
  matrix products  89.3 us (12%)
  other arithmetic  59.4 us (8%)
  loops' own time  14.4 us (2%)
  between operations  13.6 us (2%)
    all_gather x1, waiting for transfers between devices, shards(): absorb_key_rows = lax.all_gather(key_rows, 'ctx', axis=0, tiled=True)  179 us
    all_gather x1, blocking collectives, shards(): key_segments = lax.all_gather(segments, 'ctx', axis=0, tiled=True)  174 us
    psum x1, waiting for transfers between devices, shards(): lax.psum(jnp.dot(hidden, w_dkv, preferred_element_type=jnp.float32), 'head')  99.8 us
    dot_general x16, matrix products, compute(): jnp.dot(weights.astype(jnp.bfloat16).reshape(row_count * head_count, key_...  51.5 us
    dot_general x16, matrix products, compute(): lax.dot_general(query_full, key_block, (((1,), (1,)), ((), ())), preferre...  33.3 us
    convert_element_type x16, other arithmetic, compute(): weights.astype(jnp.bfloat16).reshape(row_count * head_count, key_count)  28.9 us
    squeeze x16, local copies, waits for them, and re-layouts, shards(): lax.scan(advance, initial, (absorb_key_rows.reshape(block_total, 512, KVL...  18.4 us
    unnamed x16, local copies, waits for them, and re-layouts  18 us
  transfers between devices with their start and end apart: 2, of which 2 were waited for; matrix products, arithmetic and copies ran while one was open for 1% of the time, Pallas kernels for 0%

commit v1 on v0

v1 whole, which is shorter than its diff:
```python
import functools
import math

import jax
import jax.numpy as jnp
from jax import lax
from jax.experimental import pallas as pl
from jax.experimental.pallas import tpu as pltpu
from jax.sharding import PartitionSpec as P

KVL = 512
RD = 64
NOPE = 128
VD = 128
ROPE_BASE = 10000.0
NORM_EPS = 1e-06
ROWS = 128
HEADS = 6
HIDDEN_MASK = -1e30
EXP_SCALE = math.log2(math.e) / math.sqrt(NOPE + RD)
MESH = pl.DeviceIdType.MESH
NT = (((1,), (1,)), ((), ()))
RING = (1, 3, 2)


def place(x, y, z, core):
    x, y, z = (x + 8) % 4, (y + 8) % 4, (z + 32) % 16
    return (x * 16 + y * 4 + z % 4, (z // 4) * 2 + core)


def remote(src, dst, send, recv, device):
    return pltpu.make_async_remote_copy(
        src_ref=src, dst_ref=dst, send_sem=send, recv_sem=recv, device_id=device, device_id_type=MESH
    )


def rope_tables(pos):
    lane = lax.broadcasted_iota(jnp.int32, (1, RD), 1)
    half = (lane % (RD // 2)).astype(jnp.float32)
    frequency = jnp.exp(half * (-2.0 * math.log(ROPE_BASE) / RD))
    angles = pos.astype(jnp.float32) * frequency
    sign = jnp.where(lane < RD // 2, -1.0, 1.0)
    return jnp.cos(angles), jnp.sin(angles) * sign


def rotate(v, cosine, sine):
    swapped = jnp.concatenate([v[:, RD // 2 :], v[:, : RD // 2]], axis=1)
    return v * cosine + swapped * sine


def kernel(
    hid_ref, wd_ref, gain_ref, wuk_ref, wuv_ref, q_ref, pos_ref, seg_ref, out_ref,
    lat_send, lat_recv, tot, rs_recv, key_a, key_b, key_c, qf, acc, m_s, l_s,
    s_sib, r_sib, s_rs, r_rs, s_ag, r_ag, s_p1, r_p1, s_p2, r_p2, s_p3, r_p3, s_hf, r_hf, s_sh, r_sh,
):
    ctx, head = lax.axis_index("ctx"), lax.axis_index("head")
    x, y, zl = ctx // 16, (ctx // 4) % 4, ctx % 4
    zh, c = head // 2, head % 2
    z = zh * 4 + zl
    sib = place(x, y, z, 1 - c)
    f32, bf16 = jnp.float32, jnp.bfloat16

    barrier = pltpu.get_barrier_semaphore()
    offsets = [(1, 0, 0), (2, 0, 0), (3, 0, 0), (0, 1, 0), (0, 2, 0), (0, 3, 0)]
    offsets += [(0, 0, k) for k in (1, -1, 2, -2, 4, 8, 12)]
    pl.semaphore_signal(barrier, inc=1, device_id=sib, device_id_type=MESH)
    for dx, dy, dz in offsets:
        pl.semaphore_signal(barrier, inc=1, device_id=place(x + dx, y + dy, z + dz, c), device_id_type=MESH)

    def partial(first):
        return jnp.dot(hid_ref[pl.ds(first, 64), :], wd_ref[...], preferred_element_type=f32)

    other = pl.multiple_of((1 - c) * 64, 64)
    mine = pl.multiple_of(c * 64, 64)
    lat_send[:, KVL + RD :] = jnp.zeros((64, 64), f32)
    lat_send[:, : KVL + RD] = partial(other)
    pl.semaphore_wait(barrier, 1 + len(offsets))
    swap = remote(lat_send, lat_recv, s_sib, r_sib, sib)
    swap.start()
    own = jnp.concatenate([partial(mine), jnp.zeros((64, 64), f32)], axis=1)
    swap.wait()
    tot[...] = (own + lat_recv[...]).reshape(4, 16, 640)

    rs = [
        remote(tot.at[(zh + k) % 4], rs_recv.at[k - 1], s_rs.at[k - 1], r_rs.at[k - 1], place(x, y, z + 4 * k, c))
        for k in (1, 2, 3)
    ]
    for copy in rs:
        copy.start()

    cos_q, sin_q = rope_tables(pos_ref[...])
    hide = jnp.where(seg_ref[...] == 2, HIDDEN_MASK, 0.0).astype(bf16)
    lane = lax.broadcasted_iota(jnp.int32, (ROWS, RD), 1)
    feature = jnp.where(lane == 0, hide.astype(f32), 0.0)
    for h in range(HEADS):
        base = h * (NOPE + RD)
        rows = slice(h * ROWS, (h + 1) * ROWS)
        q_nope = q_ref[:, base : base + NOPE]
        absorbed = lax.dot_general(q_nope, wuk_ref[:, h * NOPE : (h + 1) * NOPE], NT, preferred_element_type=f32)
        qf[rows, :KVL] = absorbed.astype(bf16)
        roped = rotate(q_ref[:, base + NOPE : base + NOPE + RD].astype(f32), cos_q, sin_q)
        qf[rows, KVL:] = jnp.concatenate([roped, feature], axis=1).astype(bf16)
    m_s[...] = jnp.full(m_s.shape, HIDDEN_MASK, f32)
    l_s[...] = jnp.zeros(l_s.shape, f32)
    acc[...] = jnp.zeros(acc.shape, f32)

    key_first = pl.multiple_of(c * 64 + zh * 16, 16)
    cos_k, sin_k = rope_tables(pos_ref[pl.ds(key_first, 16), :])
    seg_k = seg_ref[pl.ds(key_first, 16), :]
    lane_k = lax.broadcasted_iota(jnp.int32, (16, RD), 1)
    feature_k = jnp.where((lane_k == 0) & (seg_k == 1), 1.0, 0.0)
    for copy in rs:
        copy.wait()
    latent = tot[zh] + rs_recv[0] + rs_recv[1] + rs_recv[2]
    compressed = latent[:, :KVL]
    mean_square = jnp.mean(compressed * compressed, axis=-1, keepdims=True)
    normed = (compressed * lax.rsqrt(mean_square + NORM_EPS) * gain_ref[...]).astype(bf16)
    key_a[zh, x, c, y, zl] = normed[:, :256]
    key_b[zh, x, c, y, zl] = normed[:, 256:]
    key_c[zh, x, c, y, zl] = jnp.concatenate(
        [rotate(latent[:, KVL : KVL + RD], cos_k, sin_k), feature_k], axis=1
    ).astype(bf16)

    keys = (key_a, key_b, key_c)
    ag = []
    for k in (1, 2, 3):
        for i, key in enumerate(keys):
            ref = key.at[zh, x, c, y, zl]
            ag.append(remote(ref, ref, s_ag.at[k - 1, i], r_ag.at[k - 1, i], place(x, y, z + 4 * k, c)))
    for copy in ag:
        copy.start()

    def toward(axis, step):
        if axis == 0:
            return place(x + step, y, z, c)
        if axis == 1:
            return place(x, y + step, z, c)
        return place(x, y, z + {1: 1, 2: 2, 3: -1}[step], c)

    def phase1(m):
        copies = []
        for i, axis in enumerate((2, 2, 0)):
            ref = keys[i].at[m, x, c, y, zl]
            for k, step in enumerate(RING):
                copies.append(remote(ref, ref, s_p1.at[m, i * 3 + k], r_p1.at[m, i * 3 + k], toward(axis, step)))
        return copies

    def phase2(m):
        refs = (key_a.at[m, x, c, y], key_b.at[m, x, c, y], key_c.at[m, :, c, y, zl])
        copies = []
        for i, axis in enumerate((1, 0, 1)):
            for k, step in enumerate(RING):
                copies.append(
                    remote(refs[i], refs[i], s_p2.at[m, i * 3 + k], r_p2.at[m, i * 3 + k], toward(axis, step))
                )
        return copies

    def planes(m, d):
        return (
            key_a.at[m, (x + d) % 4, c],
            key_b.at[m, :, c, (y + d) % 4],
            key_c.at[m, :, c, :, (zl + d) % 4],
        )

    def halves(m, d, first):
        part = pl.ds(0, 2) if first else pl.ds(2, 2)
        return (
            key_a.at[m, (x + d) % 4, c, part],
            key_b.at[m, part, c, (y + d) % 4],
            key_c.at[m, part, c, :, (zl + d) % 4],
        )

    def phase3(m):
        refs = planes(m, 0)
        copies = []
        for i in range(3):
            for k, step in enumerate((1, 3)):
                copies.append(
                    remote(refs[i], refs[i], s_p3.at[m, i * 2 + k], r_p3.at[m, i * 2 + k], toward(i, step))
                )
        return copies

    def forward(m):
        copies = []
        for k, (step, back, first) in enumerate(((1, 3, True), (3, 1, False))):
            refs = halves(m, back, first)
            for i in range(3):
                copies.append(
                    remote(refs[i], refs[i], s_hf.at[m, i * 2 + k], r_hf.at[m, i * 2 + k], toward(i, step))
                )
        return copies

    def share(m, d):
        refs = planes(m, d)
        return [remote(refs[i], refs[i], s_sh.at[m, d * 3 + i], r_sh.at[m, d * 3 + i], sib) for i in range(3)]

    def start(copies):
        for copy in copies:
            copy.start()

    def wait_recv(copies):
        for copy in copies:
            copy.wait_recv()

    def wait_send(copies):
        for copy in copies:
            copy.wait_send()

    qloc = (y * 4 + zl) * ROWS

    def unit(m, xq, diagonal):
        ka = key_a[m, xq].reshape(512, 256)
        kb = key_b[m, xq].reshape(512, 256)
        kc = key_c[m, xq].reshape(512, 128)
        s = lax.dot_general(qf[...], jnp.concatenate([ka, kb, kc], axis=1), NT, preferred_element_type=f32)
        if diagonal:
            n = lax.broadcasted_iota(jnp.int32, (1, 512), 1)
            key_at = ((n >> 4) & 15) * ROWS + (n >> 8) * 64 + m * 16 + (n & 15)
            query_at = (lax.broadcasted_iota(jnp.int32, (HEADS * ROWS, 1), 0) & (ROWS - 1)) + qloc
            s = jnp.where(key_at <= query_at, s, HIDDEN_MASK)
        old = m_s[...]
        new = jnp.maximum(old, jnp.max(s, axis=1, keepdims=True))
        shrink = jnp.exp2((old - new) * EXP_SCALE)
        p = jnp.exp2((s - jnp.concatenate([new] * 4, axis=1)) * EXP_SCALE)
        l_s[...] = l_s[...] * shrink + (p[:, :128] + p[:, 128:256] + p[:, 256:384] + p[:, 384:])
        m_s[...] = new
        weights = p.astype(bf16)
        shrink = jnp.concatenate([shrink, shrink], axis=1)
        acc[:, :256] = acc[:, :256] * shrink + jnp.dot(weights, ka, preferred_element_type=f32)
        acc[:, 256:] = acc[:, 256:] * shrink + jnp.dot(weights, kb, preferred_element_type=f32)

    def attend(m):
        def full(xq, carry):
            unit(m, xq, False)
            return carry

        lax.fori_loop(0, x, full, 0)
        unit(m, x, True)

    wait_recv(ag)

    def loop(body):
        lax.fori_loop(0, 4, lambda m, carry: (body(m), carry)[1], 0)

    loop(lambda m: start(phase1(m)))

    def second(m):
        wait_recv(phase1(m))
        start(phase2(m))

    loop(second)

    def third(m):
        wait_recv(phase2(m))
        start(share(m, 0))

        @pl.when(m == 0)
        def _():
            start(phase3(m))

    loop(third)

    def stage(m, carry):
        @pl.when(m < 4)
        def _():
            wait_recv(phase3(m))

            @pl.when(m < 3)
            def _():
                start(phase3(m + 1))

            start(forward(m))
            start(share(m, 1))
            start(share(m, 3))

        @pl.when((m >= 1) & (m <= 4))
        def _():
            wait_recv(forward(m - 1))
            start(share(m - 1, 2))

        @pl.when(m >= 2)
        def _():
            for d in range(4):
                wait_recv(share(m - 2, d))
            attend(m - 2)

        return carry

    lax.fori_loop(0, 6, stage, 0)

    total = jnp.sum(l_s[...], axis=1, keepdims=True)
    for h in range(HEADS):
        rows = slice(h * ROWS, (h + 1) * ROWS)
        mixed = (acc[rows, :] / total[rows, :]).astype(bf16)
        out_ref[:, h * VD : (h + 1) * VD] = jnp.dot(
            mixed, wuv_ref[:, h * VD : (h + 1) * VD], preferred_element_type=f32
        ).astype(bf16)

    wait_send(ag)

    def finish(m):
        wait_send(phase1(m))
        wait_send(phase2(m))
        wait_send(phase3(m))
        wait_send(forward(m))
        for d in range(4):
            wait_send(share(m, d))

    loop(finish)


def shards(hidden, w_dkv, kv_gain, w_uk, w_uv, queries, segments, positions):
    f32, bf16 = jnp.float32, jnp.bfloat16
    dma = pltpu.SemaphoreType.DMA
    keys = (4, 4, 2, 4, 4, 16)
    vmem = pl.BlockSpec(memory_space=pltpu.VMEM)
    sems = [dma, dma, dma((3,)), dma((3,)), dma((3, 3)), dma((3, 3))]
    for count in (9, 9, 6, 6, 12):
        sems += [dma((4, count)), dma((4, count))]
    return pl.pallas_call(
        kernel,
        out_shape=jax.ShapeDtypeStruct((ROWS, HEADS * VD), bf16),
        in_specs=[vmem] * 8,
        out_specs=vmem,
        scratch_shapes=[
            pltpu.VMEM((64, 640), f32),
            pltpu.VMEM((64, 640), f32),
            pltpu.VMEM((4, 16, 640), f32),
            pltpu.VMEM((3, 16, 640), f32),
            pltpu.VMEM((*keys, 256), bf16),
            pltpu.VMEM((*keys, 256), bf16),
            pltpu.VMEM((*keys, 128), bf16),
            pltpu.VMEM((HEADS * ROWS, 640), bf16),
            pltpu.VMEM((HEADS * ROWS, KVL), f32),
            pltpu.VMEM((HEADS * ROWS, 128), f32),
            pltpu.VMEM((HEADS * ROWS, 128), f32),
            *sems,
        ],
        compiler_params=pltpu.CompilerParams(
            collective_id=0, has_side_effects=True, vmem_limit_bytes=56 * 2**20
        ),
    )(
        hidden, w_dkv, kv_gain.reshape(1, KVL), w_uk, w_uv, queries,
        positions.reshape(ROWS, 1), segments.reshape(ROWS, 1),
    )


def solution(mesh):
    in_specs = (
        P("ctx", "head"),
        P("head", None),
        P(),
        P(None, "head"),
        P(None, "head"),
        P("ctx", "head"),
        P("ctx"),
        P("ctx"),
    )
    out_specs = P("ctx", "head")
    return jax.shard_map(shards, mesh=mesh, in_specs=in_specs, out_specs=out_specs, check_vma=False)
```

time: 728 us -> 99.3 us (0.14)
  the two profiles are of different devices: /device:TPU:94 before, /device:TPU:38 now
where the time goes in v1:
time: 99.3 us; the launch traced here: 99.1 us
  Pallas kernels  92.4 us (93%)
  local copies, waits for them, and re-layouts  6.73 us (7%)
    pallas_call x1, Pallas kernels, shards(): pl.pallas_call(kernel, out_shape=jax.ShapeDtypeStruct((ROWS, HEADS * VD),...  92.4 us
    unnamed x2, local copies, waits for them, and re-layouts  3.96 us

profile of v1, /device:TPU:38, one launch (start us, length us, event | category | flops | bytes accessed | tf_op | source)
XLA Modules:
  0.0 99.1 jit_solution(16341566956443962671)
XLA Ops:
  0.0 1.4 %copy.11.seg_ref = s32[128,1]{1,0:T(8,128)} copy(s32[128,1]{0,1:T(1,128)} %bitcast.4) | data formatting | bytes 1024 | tf_op jit(solution)/shard_map/reshape | solution.py:344
  1.4 1.4 %copy.10.pos_ref = s32[128,1]{1,0:T(8,128)} copy(s32[128,1]{0,1:T(1,128)} %bitcast.5) | data formatting | bytes 1024 | tf_op jit(solution)/shard_map/reshape | solution.py:344
  2.8 2.3 %copy.9.wd_ref = bf16[896,576]{1,0:T(8,128)(2,1)} copy(bf16[896,576]{0,1:T(8,128)(2,1)} %param.9) | data formatting | bytes 2064384 | tf_op args[1]
  5.1 92.4 %shard_map.82 = bf16[128,768]{1,0:T(8,128)(2,1)} custom-call(bf16[128,896]{1,0:T(8,128)(2,1)} %hid_ref.1, bf16[896,576]{1,0:T(8,128)(2,1)} %copy.9.wd_ref, f32[1,512]{1,0:T(1,128)} %bitcast.3, bf16[512,768]{1,0:T(8,128)(2,1)} %wuk_ref.1, bf16[512,768]{1,0:T(8,128)(2,1)} %wuv_ref.1, bf16[128,1152]{1,0:T(8,128)(2,1)} %q_ref.1, s32[128,1]{1,0:T(8,128)} %copy.10.pos_ref, ...), custom_call_target="tpu_custom_call" | custom-call | tf_op jit(solution)/shard_map/pallas_call | solution.py:320
  97.5 1.6 %copy.13 = bf16[128,768]{1,0:T(8,128)(2,1)} copy(bf16[128,768]{1,0:T(8,128)(2,1)} %shard_map.82) | data formatting | bytes 393216

commit v2 on v1

v2 whole, which is shorter than its diff:
```python
import functools
import math

import jax
import jax.numpy as jnp
from jax import lax
from jax.experimental import pallas as pl
from jax.experimental.pallas import tpu as pltpu
from jax.sharding import PartitionSpec as P

KVL = 512
RD = 64
NOPE = 128
VD = 128
ROPE_BASE = 10000.0
NORM_EPS = 1e-06
ROWS = 128
HEADS = 6
HIDDEN_MASK = -1e30
EXP_SCALE = math.log2(math.e) / math.sqrt(NOPE + RD)
MESH = pl.DeviceIdType.MESH
NT = (((1,), (1,)), ((), ()))
RING = (1, 3, 2)
WIDTH = 640


def place(x, y, z, core):
    x, y, z = (x + 8) % 4, (y + 8) % 4, (z + 32) % 16
    return (x * 16 + y * 4 + z % 4, (z // 4) * 2 + core)


def remote(src, dst, send, recv, device):
    return pltpu.make_async_remote_copy(
        src_ref=src, dst_ref=dst, send_sem=send, recv_sem=recv, device_id=device, device_id_type=MESH
    )


def rope_tables(pos):
    lane = lax.broadcasted_iota(jnp.int32, (1, RD), 1)
    half = (lane % (RD // 2)).astype(jnp.float32)
    frequency = jnp.exp(half * (-2.0 * math.log(ROPE_BASE) / RD))
    angles = pos.astype(jnp.float32) * frequency
    sign = jnp.where(lane < RD // 2, -1.0, 1.0)
    return jnp.cos(angles), jnp.sin(angles) * sign


def rotate(v, cosine, sine):
    swapped = jnp.concatenate([v[:, RD // 2 :], v[:, : RD // 2]], axis=1)
    return v * cosine + swapped * sine


def column(row):
    n = row.shape[1]
    at = lax.broadcasted_iota(jnp.int32, (n, n), 0) == lax.broadcasted_iota(jnp.int32, (n, n), 1)
    return jnp.sum(jnp.where(at, row.astype(jnp.float32), 0.0), axis=1, keepdims=True)


def kernel(
    hid_hbm, wd_hbm, gain_ref, wuk_hbm, wuv_hbm, q_hbm, pos_ref, seg_ref, out_ref,
    hid_ref, wd_ref, wuk_ref, wuv_ref, q_ref, pos_s, seg_s,
    lat_send, lat_recv, tot, rs_recv, keys, qf, acc, m_s, l_s,
    s_in, s_sib, r_sib, s_rs, r_rs, s_ag, r_ag, s_p1, r_p1, s_p2, r_p2, s_p3, r_p3, s_fw, r_fw, s_sh, r_sh,
):
    ctx, head = lax.axis_index("ctx"), lax.axis_index("head")
    x, y, zl = ctx // 16, (ctx // 4) % 4, ctx % 4
    zh, c = head // 2, head % 2
    z = zh * 4 + zl
    sib = place(x, y, z, 1 - c)
    f32, bf16 = jnp.float32, jnp.bfloat16

    loads = [
        pltpu.make_async_copy(src, dst, s_in.at[i])
        for i, (src, dst) in enumerate(
            ((hid_hbm, hid_ref), (wd_hbm, wd_ref), (q_hbm, q_ref), (wuk_hbm, wuk_ref), (wuv_hbm, wuv_ref))
        )
    ]
    for load in loads:
        load.start()

    barrier = pltpu.get_barrier_semaphore()
    offsets = [(1, 0, 0), (2, 0, 0), (3, 0, 0), (0, 1, 0), (0, 2, 0), (0, 3, 0)]
    offsets += [(0, 0, k) for k in (1, -1, 2, -2, 4, 8, 12)]
    pl.semaphore_signal(barrier, inc=1, device_id=sib, device_id_type=MESH)
    for dx, dy, dz in offsets:
        pl.semaphore_signal(barrier, inc=1, device_id=place(x + dx, y + dy, z + dz, c), device_id_type=MESH)

    def partial(first):
        return lax.dot_general(hid_ref[pl.ds(first, 64), :], wd_ref[...], NT, preferred_element_type=f32)

    other = pl.multiple_of((1 - c) * 64, 64)
    mine = pl.multiple_of(c * 64, 64)
    lat_send[:, KVL + RD :] = jnp.zeros((64, 64), f32)
    loads[0].wait()
    loads[1].wait()
    lat_send[:, : KVL + RD] = partial(other)
    pl.semaphore_wait(barrier, 1 + len(offsets))
    swap = remote(lat_send, lat_recv, s_sib, r_sib, sib)
    swap.start()
    own = jnp.concatenate([partial(mine), jnp.zeros((64, 64), f32)], axis=1)
    swap.wait()
    tot[...] = (own + lat_recv[...]).reshape(4, 16, WIDTH)

    rs = [
        remote(tot.at[(zh + k) % 4], rs_recv.at[k - 1], s_rs.at[k - 1], r_rs.at[k - 1], place(x, y, z + 4 * k, c))
        for k in (1, 2, 3)
    ]
    for copy in rs:
        copy.start()

    pos_s[...] = column(pos_ref[...])
    seg_s[...] = column(seg_ref[...])
    cos_q, sin_q = rope_tables(pos_s[...])
    lane = lax.broadcasted_iota(jnp.int32, (ROWS, RD), 1)
    feature = jnp.where((lane == 0) & (seg_s[...] == 2.0), HIDDEN_MASK, 0.0)
    loads[2].wait()
    loads[3].wait()
    for h in range(HEADS):
        base = h * (NOPE + RD)
        rows = slice(h * ROWS, (h + 1) * ROWS)
        q_nope = q_ref[:, base : base + NOPE]
        absorbed = lax.dot_general(q_nope, wuk_ref[:, h * NOPE : (h + 1) * NOPE], NT, preferred_element_type=f32)
        qf[rows, :KVL] = absorbed.astype(bf16)
        roped = rotate(q_ref[:, base + NOPE : base + NOPE + RD].astype(f32), cos_q, sin_q)
        qf[rows, KVL:] = jnp.concatenate([roped, feature], axis=1).astype(bf16)
    m_s[...] = jnp.full(m_s.shape, HIDDEN_MASK, f32)
    l_s[...] = jnp.zeros(l_s.shape, f32)
    acc[...] = jnp.zeros(acc.shape, f32)

    key_first = pl.multiple_of(c * 64 + zh * 16, 16)
    cos_k, sin_k = rope_tables(pos_s[pl.ds(key_first, 16), :])
    seg_k = seg_s[pl.ds(key_first, 16), :]
    lane_k = lax.broadcasted_iota(jnp.int32, (16, RD), 1)
    feature_k = jnp.where((lane_k == 0) & (seg_k == 1.0), 1.0, 0.0)
    for copy in rs:
        copy.wait()
    latent = tot[zh] + rs_recv[0] + rs_recv[1] + rs_recv[2]
    compressed = latent[:, :KVL]
    mean_square = jnp.mean(compressed * compressed, axis=-1, keepdims=True)
    normed = compressed * lax.rsqrt(mean_square + NORM_EPS) * gain_ref[...]
    roped_k = rotate(latent[:, KVL : KVL + RD], cos_k, sin_k)
    keys[zh, x, c, y, zl] = jnp.concatenate([normed, roped_k, feature_k], axis=1).astype(bf16)

    piece = keys.at[zh, x, c, y, zl]
    ag = [remote(piece, piece, s_ag.at[k - 1], r_ag.at[k - 1], place(x, y, z + 4 * k, c)) for k in (1, 2, 3)]
    for copy in ag:
        copy.start()

    def toward(axis, step):
        if axis == 0:
            return place(x + step, y, z, c)
        if axis == 1:
            return place(x, y + step, z, c)
        return place(x, y, z + {1: 1, 2: 2, 3: -1}[step], c)

    first_axis, second_axis = (2, 0, 1), (1, 2, 0)
    block = {
        0: lambda m: keys.at[m, x, c, y],
        1: lambda m: keys.at[m, :, c, y, zl],
        2: lambda m: keys.at[m, x, c, :, zl],
    }
    plane = {
        0: lambda m, d, part: keys.at[m, (x + d) % 4, c, part],
        1: lambda m, d, part: keys.at[m, part, c, (y + d) % 4],
        2: lambda m, d, part: keys.at[m, part, c, :, (zl + d) % 4],
    }
    low, high, whole = pl.ds(0, 2), pl.ds(2, 2), pl.ds(0, 4)

    def phase1(kind, m):
        ref = keys.at[m, x, c, y, zl]
        return [
            remote(ref, ref, s_p1.at[m, k], r_p1.at[m, k], toward(first_axis[kind], step))
            for k, step in enumerate(RING)
        ]

    def phase2(kind, m):
        ref = block[kind](m)
        return [
            remote(ref, ref, s_p2.at[m, k], r_p2.at[m, k], toward(second_axis[kind], step))
            for k, step in enumerate(RING)
        ]

    def phase3(kind, m, turn):
        copies = []
        for k, (step, parts) in enumerate(((1, (low, high)), (3, (high, low)))):
            ref = plane[kind](m, 0, parts[turn])
            copies.append(remote(ref, ref, s_p3.at[m, k * 2 + turn], r_p3.at[m, k * 2 + turn], toward(kind, step)))
        return copies

    def forward(kind, m):
        copies = []
        for k, (step, back, part) in enumerate(((1, 3, low), (3, 1, high))):
            ref = plane[kind](m, back, part)
            copies.append(remote(ref, ref, s_fw.at[m, k], r_fw.at[m, k], toward(kind, step)))
        return copies

    def share(kind, m, d):
        ref = plane[kind](m, d, whole)
        return [remote(ref, ref, s_sh.at[m, d], r_sh.at[m, d], sib)]

    def start(copies):
        for copy in copies:
            copy.start()

    def wait_recv(copies):
        for copy in copies:
            copy.wait_recv()

    def wait_send(copies):
        for copy in copies:
            copy.wait_send()

    def each(task, *sets):
        for m in sets:
            if m < 3:
                task(m, m)
            else:
                for kind in (0, 1):
                    pl.when(c == kind)(functools.partial(task, kind, m))

    def one(kind, m):
        start(phase1(kind, m))

    def two(kind, m):
        wait_recv(phase1(kind, m))
        start(phase2(kind, m))

    def three(kind, m):
        wait_recv(phase2(kind, m))
        start(share(kind, m, 0))
        if m < 3:
            four(kind, m)

    def four(kind, m):
        start(phase3(kind, m, 0))
        start(phase3(kind, m, 1))

    def five(kind, m):
        wait_recv(phase3(kind, m, 0))
        start(forward(kind, m))

    def six(kind, m):
        wait_recv(phase3(kind, m, 1))
        start(share(kind, m, 1))
        start(share(kind, m, 3))

    def seven(kind, m):
        wait_recv(forward(kind, m))
        start(share(kind, m, 2))

    query_at = (lax.broadcasted_iota(jnp.int32, (HEADS * ROWS, 1), 0) & (ROWS - 1)) + ctx * ROWS
    n = lax.broadcasted_iota(jnp.int32, (1, 512), 1)

    def unit(k, key_at):
        s = lax.dot_general(qf[...], k, NT, preferred_element_type=f32)
        s = jnp.where(key_at <= query_at, s, HIDDEN_MASK)
        old = m_s[...]
        new = jnp.maximum(old, jnp.max(s, axis=1, keepdims=True))
        shrink = jnp.exp2((old - new) * EXP_SCALE)
        p = jnp.exp2((s - jnp.concatenate([new] * 4, axis=1)) * EXP_SCALE)
        l_s[...] = l_s[...] * shrink + (p[:, :128] + p[:, 128:256] + p[:, 256:384] + p[:, 384:])
        m_s[...] = new
        update = jnp.dot(p.astype(bf16), k[:, :KVL], preferred_element_type=f32)
        acc[...] = acc[...] * jnp.concatenate([shrink] * 4, axis=1) + update

    def unit_x(m, xq):
        @pl.when(xq <= x)
        def _():
            at = (xq * 16 + ((n >> 4) & 15)) * ROWS + (n >> 8) * 64 + m * 16 + (n & 15)
            unit(keys[m, xq].reshape(512, WIDTH), at)

    def unit_y(m, yq):
        at = ((n >> 7) * 16 + yq * 4 + ((n >> 4) & 3)) * ROWS + ((n >> 6) & 1) * 64 + m * 16 + (n & 15)
        unit(keys[m, :, :, yq].reshape(512, WIDTH), at)

    def unit_z(m, zq):
        at = ((n >> 7) * 16 + ((n >> 4) & 3) * 4 + zq) * ROWS + ((n >> 6) & 1) * 64 + m * 16 + (n & 15)
        unit(keys[m, :, :, :, zq].reshape(512, WIDTH), at)

    wait_recv(ag)
    each(one, 0, 1, 2, 3)
    each(two, 0, 1, 2, 3)
    each(three, 0, 1, 2, 3)

    def step(t, carry):
        d = jnp.where(t < 2, t, 5 - t)
        joint = t < 4

        @pl.when(t == 1)
        def _():
            each(five, 0, 1, 2)
            each(six, 0, 1, 2)
            each(four, 3)

        @pl.when(t == 2)
        def _():
            each(seven, 0, 1, 2)

        @pl.when(t == 3)
        def _():
            each(six, 3)

        @pl.when(t == 4)
        def _():
            for k in range(4):
                wait_recv(share(0, 3, k))

        @pl.when(joint)
        def _():
            wait_recv(share(0, 0, d))

        unit_x(jnp.where(joint, 0, 3), jnp.where(joint, (x + d) % 4, t - 4))

        @pl.when(joint)
        def _():
            wait_recv(share(1, 1, d))
            unit_y(1, (y + d) % 4)

            @pl.when(t == 2)
            def _():
                each(five, 3)

            @pl.when(t == 3)
            def _():
                each(seven, 3)

            wait_recv(share(2, 2, d))
            unit_z(2, (zl + d) % 4)

        return carry

    lax.fori_loop(0, 8, step, 0)

    loads[4].wait()
    total = jnp.sum(l_s[...], axis=1, keepdims=True)
    for h in range(HEADS):
        rows = slice(h * ROWS, (h + 1) * ROWS)
        mixed = (acc[rows, :] / total[rows, :]).astype(bf16)
        out_ref[:, h * VD : (h + 1) * VD] = jnp.dot(
            mixed, wuv_ref[:, h * VD : (h + 1) * VD], preferred_element_type=f32
        ).astype(bf16)

    wait_send(ag)

    def finish(kind, m):
        wait_send(phase1(kind, m) + phase2(kind, m) + phase3(kind, m, 0) + phase3(kind, m, 1) + forward(kind, m))
        for d in range(4):
            wait_send(share(kind, m, d))

    each(finish, 0, 1, 2, 3)


def shards(hidden, w_dkv, kv_gain, w_uk, w_uv, queries, segments, positions):
    f32, bf16 = jnp.float32, jnp.bfloat16
    dma = pltpu.SemaphoreType.DMA
    vmem = pl.BlockSpec(memory_space=pltpu.VMEM)
    hbm = pl.BlockSpec(memory_space=pl.ANY)
    sems = [dma((5,)), dma, dma, dma((3,)), dma((3,)), dma((3,)), dma((3,))]
    for count in (3, 3, 4, 2, 4):
        sems += [dma((4, count)), dma((4, count))]
    operands = (hidden, w_dkv.T, w_uk, w_uv, queries)
    return pl.pallas_call(
        kernel,
        out_shape=jax.ShapeDtypeStruct((ROWS, HEADS * VD), bf16),
        in_specs=[hbm, hbm, vmem, hbm, hbm, hbm, vmem, vmem],
        out_specs=vmem,
        scratch_shapes=[
            *[pltpu.VMEM(a.shape, a.dtype) for a in operands],
            pltpu.VMEM((ROWS, 1), f32),
            pltpu.VMEM((ROWS, 1), f32),
            pltpu.VMEM((64, WIDTH), f32),
            pltpu.VMEM((64, WIDTH), f32),
            pltpu.VMEM((4, 16, WIDTH), f32),
            pltpu.VMEM((3, 16, WIDTH), f32),
            pltpu.VMEM((4, 4, 2, 4, 4, 16, WIDTH), bf16),
            pltpu.VMEM((HEADS * ROWS, WIDTH), bf16),
            pltpu.VMEM((HEADS * ROWS, KVL), f32),
            pltpu.VMEM((HEADS * ROWS, 128), f32),
            pltpu.VMEM((HEADS * ROWS, 128), f32),
            *sems,
        ],
        compiler_params=pltpu.CompilerParams(
            collective_id=0, has_side_effects=True, vmem_limit_bytes=56 * 2**20
        ),
    )(
        operands[0], operands[1], kv_gain.reshape(1, KVL), *operands[2:],
        positions.reshape(1, ROWS), segments.reshape(1, ROWS),
    )


def solution(mesh):
    in_specs = (
        P("ctx", "head"),
        P("head", None),
        P(),
        P(None, "head"),
        P(None, "head"),
        P("ctx", "head"),
        P("ctx"),
        P("ctx"),
    )
    out_specs = P("ctx", "head")
    return jax.shard_map(shards, mesh=mesh, in_specs=in_specs, out_specs=out_specs, check_vma=False)
```

time: 99.3 us -> 79.3 us (0.80)
  the two profiles are of different devices: /device:TPU:38 before, /device:TPU:7 now
where the time goes in v2:
time: 79.3 us; the launch traced here: 79.1 us
  Pallas kernels  77.5 us (98%)
  local copies, waits for them, and re-layouts  1.62 us (2%)
    pallas_call x1, Pallas kernels, shards(): pl.pallas_call(kernel, out_shape=jax.ShapeDtypeStruct((ROWS, HEADS * VD),...  77.5 us
    unnamed x1, local copies, waits for them, and re-layouts  1.62 us

profile of v2, /device:TPU:7, one launch (start us, length us, event | category | flops | bytes accessed | tf_op | source)
XLA Modules:
  0.0 79.1 jit_solution(13697183202221007255)
XLA Ops:
  0.0 77.5 %shard_map.82 = bf16[128,768]{1,0:T(8,128)(2,1)} custom-call(bf16[128,896]{1,0:T(8,128)(2,1)} %hid_hbm.1, bf16[576,896]{1,0:T(8,128)(2,1)} %bitcast.4, f32[1,512]{1,0:T(1,128)} %bitcast.5, bf16[512,768]{1,0:T(8,128)(2,1)} %wuk_hbm.1, bf16[512,768]{1,0:T(8,128)(2,1)} %wuv_hbm.1, bf16[128,1152]{1,0:T(8,128)(2,1)} %q_hbm.1, s32[1,128]{1,0:T(1,128)} %bitcast.6, ...), custom_call_target="tpu_custom_call" | custom-call | tf_op jit(solution)/shard_map/pallas_call | solution.py:361
  77.5 1.6 %copy.10 = bf16[128,768]{1,0:T(8,128)(2,1)} copy(bf16[128,768]{1,0:T(8,128)(2,1)} %shard_map.82) | data formatting | bytes 393216

commit v3 on v2

--- a/solution.py
+++ b/solution.py
@@ -56,9 +56,9 @@
 
 
 def kernel(
-    hid_hbm, wd_hbm, gain_ref, wuk_hbm, wuv_hbm, q_hbm, pos_ref, seg_ref, out_ref,
-    hid_ref, wd_ref, wuk_ref, wuv_ref, q_ref, pos_s, seg_s,
-    lat_send, lat_recv, tot, rs_recv, keys, qf, acc, m_s, l_s,
+    hid_hbm, wd_hbm, gain_hbm, wuk_hbm, wuv_hbm, q_hbm, pos_hbm, seg_hbm, out_ref,
+    hid_ref, wd_ref, wuk_ref, wuv_ref, q_ref, gain_ref, pos_ref, seg_ref, pos_s, seg_s,
+    lat_send, lat_recv, tot, tot_rope, rs_recv, rs_rope, keys, qf, acc, m_s, l_s,
     s_in, s_sib, r_sib, s_rs, r_rs, s_ag, r_ag, s_p1, r_p1, s_p2, r_p2, s_p3, r_p3, s_fw, r_fw, s_sh, r_sh,
 ):
     ctx, head = lax.axis_index("ctx"), lax.axis_index("head")
@@ -71,10 +71,16 @@
     loads = [
         pltpu.make_async_copy(src, dst, s_in.at[i])
         for i, (src, dst) in enumerate(
-            ((hid_hbm, hid_ref), (wd_hbm, wd_ref), (q_hbm, q_ref), (wuk_hbm, wuk_ref), (wuv_hbm, wuv_ref))
+            (
+                (hid_hbm, hid_ref), (q_hbm, q_ref), (wuk_hbm, wuk_ref), (wuv_hbm, wuv_ref),
+                (gain_hbm, gain_ref), (pos_hbm, pos_ref), (seg_hbm, seg_ref),
+            )
         )
     ]
-    for load in loads:
+    first_loads = [
+        pltpu.make_async_copy(wd_hbm.at[pl.ds(144 * i, 144)], wd_ref.at[pl.ds(144 * i, 144)], s_in.at[7 + i]) for i in range(4)
+    ]
+    for load in loads[:1] + first_loads:
         load.start()
 
     barrier = pltpu.get_barrier_semaphore()
@@ -91,29 +97,59 @@
     mine = pl.multiple_of(c * 64, 64)
     lat_send[:, KVL + RD :] = jnp.zeros((64, 64), f32)
     loads[0].wait()
-    loads[1].wait()
+    for load in first_loads:
+        load.wait()
     lat_send[:, : KVL + RD] = partial(other)
     pl.semaphore_wait(barrier, 1 + len(offsets))
     swap = remote(lat_send, lat_recv, s_sib, r_sib, sib)
     swap.start()
+    for load in loads[1:]:
+        load.start()
     own = jnp.concatenate([partial(mine), jnp.zeros((64, 64), f32)], axis=1)
     swap.wait()
-    tot[...] = (own + lat_recv[...]).reshape(4, 16, WIDTH)
-
-    rs = [
-        remote(tot.at[(zh + k) % 4], rs_recv.at[k - 1], s_rs.at[k - 1], r_rs.at[k - 1], place(x, y, z + 4 * k, c))
-        for k in (1, 2, 3)
-    ]
+    total_rows = own + lat_recv[...]
+    tot[...] = total_rows[:, :KVL].reshape(4, 16, KVL)
+    for i in range(4):
+        rope_rows = total_rows[i * 16 : (i + 1) * 16, KVL : KVL + RD]
+        tot_rope[i] = jnp.concatenate([rope_rows[:8], rope_rows[8:]], axis=1)
+
+    rs = []
+    for k in (1, 2, 3):
+        for i, (src, dst) in enumerate(((tot, rs_recv), (tot_rope, rs_rope))):
+            peer = place(x, y, z + 4 * k, c)
+            rs.append(remote(src.at[(zh + k) % 4], dst.at[k - 1], s_rs.at[k - 1, i], r_rs.at[k - 1, i], peer))
     for copy in rs:
         copy.start()
 
+    for load in loads[4:]:
+        load.wait()
     pos_s[...] = column(pos_ref[...])
     seg_s[...] = column(seg_ref[...])
+    key_first = pl.multiple_of(c * 64 + zh * 16, 16)
+    cos_k, sin_k = rope_tables(pos_s[pl.ds(key_first, 16), :])
+    seg_k = seg_s[pl.ds(key_first, 16), :]
+    lane_k = lax.broadcasted_iota(jnp.int32, (16, RD), 1)
+    feature_k = jnp.where((lane_k == 0) & (seg_k == 1.0), 1.0, 0.0)
+    for copy in rs:
+        copy.wait()
+    compressed = tot[zh] + rs_recv[0] + rs_recv[1] + rs_recv[2]
+    rope_k = tot_rope[zh] + rs_rope[0] + rs_rope[1] + rs_rope[2]
+    rope_k = jnp.concatenate([rope_k[:, :RD], rope_k[:, RD:]], axis=0)
+    mean_square = jnp.mean(compressed * compressed, axis=-1, keepdims=True)
+    normed = compressed * lax.rsqrt(mean_square + NORM_EPS) * gain_ref[...]
+    roped_k = rotate(rope_k, cos_k, sin_k)
+    keys[zh, x, c, y, zl] = jnp.concatenate([normed, roped_k, feature_k], axis=1).astype(bf16)
+
+    piece = keys.at[zh, x, c, y, zl]
+    ag = [remote(piece, piece, s_ag.at[k - 1], r_ag.at[k - 1], place(x, y, z + 4 * k, c)) for k in (1, 2, 3)]
+    for copy in ag:
+        copy.start()
+
     cos_q, sin_q = rope_tables(pos_s[...])
     lane = lax.broadcasted_iota(jnp.int32, (ROWS, RD), 1)
     feature = jnp.where((lane == 0) & (seg_s[...] == 2.0), HIDDEN_MASK, 0.0)
+    loads[1].wait()
     loads[2].wait()
-    loads[3].wait()
     for h in range(HEADS):
         base = h * (NOPE + RD)
         rows = slice(h * ROWS, (h + 1) * ROWS)
@@ -126,31 +162,14 @@
     l_s[...] = jnp.zeros(l_s.shape, f32)
     acc[...] = jnp.zeros(acc.shape, f32)
 
-    key_first = pl.multiple_of(c * 64 + zh * 16, 16)
-    cos_k, sin_k = rope_tables(pos_s[pl.ds(key_first, 16), :])
-    seg_k = seg_s[pl.ds(key_first, 16), :]
-    lane_k = lax.broadcasted_iota(jnp.int32, (16, RD), 1)
-    feature_k = jnp.where((lane_k == 0) & (seg_k == 1.0), 1.0, 0.0)
-    for copy in rs:
-        copy.wait()
-    latent = tot[zh] + rs_recv[0] + rs_recv[1] + rs_recv[2]
-    compressed = latent[:, :KVL]
-    mean_square = jnp.mean(compressed * compressed, axis=-1, keepdims=True)
-    normed = compressed * lax.rsqrt(mean_square + NORM_EPS) * gain_ref[...]
-    roped_k = rotate(latent[:, KVL : KVL + RD], cos_k, sin_k)
-    keys[zh, x, c, y, zl] = jnp.concatenate([normed, roped_k, feature_k], axis=1).astype(bf16)
-
-    piece = keys.at[zh, x, c, y, zl]
-    ag = [remote(piece, piece, s_ag.at[k - 1], r_ag.at[k - 1], place(x, y, z + 4 * k, c)) for k in (1, 2, 3)]
-    for copy in ag:
-        copy.start()
+    across = jnp.where(zl % 2 == 0, 2, -2)
 
     def toward(axis, step):
         if axis == 0:
             return place(x + step, y, z, c)
         if axis == 1:
             return place(x, y + step, z, c)
-        return place(x, y, z + {1: 1, 2: 2, 3: -1}[step], c)
+        return place(x, y, z + {1: 1, 2: across, 3: -1}[step], c)
 
     first_axis, second_axis = (2, 0, 1), (1, 2, 0)
     block = {
@@ -165,17 +184,22 @@
     }
     low, high, whole = pl.ds(0, 2), pl.ds(2, 2), pl.ds(0, 4)
 
+    def route(kind, m):
+        if (kind, m) == (0, 3):
+            return 1, 2, block[2](m)
+        return first_axis[kind], second_axis[kind], block[kind](m)
+
     def phase1(kind, m):
         ref = keys.at[m, x, c, y, zl]
         return [
-            remote(ref, ref, s_p1.at[m, k], r_p1.at[m, k], toward(first_axis[kind], step))
+            remote(ref, ref, s_p1.at[m, k], r_p1.at[m, k], toward(route(kind, m)[0], step))
             for k, step in enumerate(RING)
         ]
 
     def phase2(kind, m):
-        ref = block[kind](m)
+        _, axis, ref = route(kind, m)
         return [
-            remote(ref, ref, s_p2.at[m, k], r_p2.at[m, k], toward(second_axis[kind], step))
+            remote(ref, ref, s_p2.at[m, k], r_p2.at[m, k], toward(axis, step))
             for k, step in enumerate(RING)
         ]
 
@@ -276,65 +300,64 @@
         at = ((n >> 7) * 16 + ((n >> 4) & 3) * 4 + zq) * ROWS + ((n >> 6) & 1) * 64 + m * 16 + (n & 15)
         unit(keys[m, :, :, :, zq].reshape(512, WIDTH), at)
 
+    def unit_3(d):
+        xq, yq = (x + d) % 4, (y + d) % 4
+        half = n & 255
+        at_0 = (xq * 16 + (half >> 4)) * ROWS
+        at_1 = ((half >> 6) * 16 + yq * 4 + ((half >> 4) & 3)) * ROWS + 64
+        k = jnp.concatenate([keys[3, xq, 0].reshape(256, WIDTH), keys[3, :, 1, yq].reshape(256, WIDTH)], axis=0)
+        unit(k, jnp.where(n < 256, at_0, at_1) + 3 * 16 + (n & 15))
+
     wait_recv(ag)
     each(one, 0, 1, 2, 3)
     each(two, 0, 1, 2, 3)
     each(three, 0, 1, 2, 3)
 
-    def step(t, carry):
-        d = jnp.where(t < 2, t, 5 - t)
-        joint = t < 4
-
-        @pl.when(t == 1)
-        def _():
-            each(five, 0, 1, 2)
-            each(six, 0, 1, 2)
-            each(four, 3)
-
-        @pl.when(t == 2)
-        def _():
-            each(seven, 0, 1, 2)
-
-        @pl.when(t == 3)
-        def _():
-            each(six, 3)
-
-        @pl.when(t == 4)
-        def _():
-            for k in range(4):
-                wait_recv(share(0, 3, k))
-
-        @pl.when(joint)
-        def _():
-            wait_recv(share(0, 0, d))
-
-        unit_x(jnp.where(joint, 0, 3), jnp.where(joint, (x + d) % 4, t - 4))
-
-        @pl.when(joint)
-        def _():
-            wait_recv(share(1, 1, d))
-            unit_y(1, (y + d) % 4)
-
-            @pl.when(t == 2)
-            def _():
-                each(five, 3)
-
-            @pl.when(t == 3)
-            def _():
-                each(seven, 3)
-
-            wait_recv(share(2, 2, d))
-            unit_z(2, (zl + d) % 4)
-
-        return carry
-
-    lax.fori_loop(0, 8, step, 0)
-
-    loads[4].wait()
-    total = jnp.sum(l_s[...], axis=1, keepdims=True)
+    wait_recv(share(0, 0, 0))
+    unit_x(0, (x + 0) % 4)
+    wait_recv(share(1, 1, 0))
+    unit_y(1, (y + 0) % 4)
+    wait_recv(share(2, 2, 0))
+    unit_z(2, (zl + 0) % 4)
+    each(five, 0, 1, 2)
+    each(four, 3)
+    wait_recv(share(0, 3, 0))
+    unit_3(0)
+    each(six, 0, 1, 2)
+    wait_recv(share(0, 0, 1))
+    unit_x(0, (x + 1) % 4)
+    wait_recv(share(1, 1, 1))
+    unit_y(1, (y + 1) % 4)
+    wait_recv(share(2, 2, 1))
+    unit_z(2, (zl + 1) % 4)
+    each(five, 3)
+    wait_recv(share(0, 0, 3))
+    unit_x(0, (x + 3) % 4)
+    each(seven, 0, 1, 2)
+    wait_recv(share(1, 1, 3))
+    unit_y(1, (y + 3) % 4)
+    each(six, 3)
+    wait_recv(share(2, 2, 3))
+    unit_z(2, (zl + 3) % 4)
+    wait_recv(share(0, 0, 2))
+    unit_x(0, (x + 2) % 4)
+    wait_recv(share(1, 1, 2))
+    unit_y(1, (y + 2) % 4)
+    each(seven, 3)
+    wait_recv(share(2, 2, 2))
+    unit_z(2, (zl + 2) % 4)
+    wait_recv(share(0, 3, 1))
+    unit_3(1)
+    wait_recv(share(0, 3, 3))
+    unit_3(3)
+    wait_recv(share(0, 3, 2))
+    unit_3(2)
+
+    loads[3].wait()
+    inverse = 1.0 / jnp.sum(l_s[...], axis=1, keepdims=True)
     for h in range(HEADS):
         rows = slice(h * ROWS, (h + 1) * ROWS)
-        mixed = (acc[rows, :] / total[rows, :]).astype(bf16)
+        mixed = (acc[rows, :] * inverse[rows, :]).astype(bf16)
         out_ref[:, h * VD : (h + 1) * VD] = jnp.dot(
             mixed, wuv_ref[:, h * VD : (h + 1) * VD], preferred_element_type=f32
         ).astype(bf16)
@@ -354,23 +377,28 @@
     dma = pltpu.SemaphoreType.DMA
     vmem = pl.BlockSpec(memory_space=pltpu.VMEM)
     hbm = pl.BlockSpec(memory_space=pl.ANY)
-    sems = [dma((5,)), dma, dma, dma((3,)), dma((3,)), dma((3,)), dma((3,))]
+    sems = [dma((11,)), dma, dma, dma((3, 2)), dma((3, 2)), dma((3,)), dma((3,))]
     for count in (3, 3, 4, 2, 4):
         sems += [dma((4, count)), dma((4, count))]
     operands = (hidden, w_dkv.T, w_uk, w_uv, queries)
     return pl.pallas_call(
         kernel,
         out_shape=jax.ShapeDtypeStruct((ROWS, HEADS * VD), bf16),
-        in_specs=[hbm, hbm, vmem, hbm, hbm, hbm, vmem, vmem],
+        in_specs=[hbm] * 8,
         out_specs=vmem,
         scratch_shapes=[
             *[pltpu.VMEM(a.shape, a.dtype) for a in operands],
+            pltpu.VMEM((1, KVL), f32),
+            pltpu.VMEM((1, ROWS), jnp.int32),
+            pltpu.VMEM((1, ROWS), jnp.int32),
             pltpu.VMEM((ROWS, 1), f32),
             pltpu.VMEM((ROWS, 1), f32),
             pltpu.VMEM((64, WIDTH), f32),
             pltpu.VMEM((64, WIDTH), f32),
-            pltpu.VMEM((4, 16, WIDTH), f32),
-            pltpu.VMEM((3, 16, WIDTH), f32),
+            pltpu.VMEM((4, 16, KVL), f32),
+            pltpu.VMEM((4, 8, 2 * RD), f32),
+            pltpu.VMEM((3, 16, KVL), f32),
+            pltpu.VMEM((3, 8, 2 * RD), f32),
             pltpu.VMEM((4, 4, 2, 4, 4, 16, WIDTH), bf16),
             pltpu.VMEM((HEADS * ROWS, WIDTH), bf16),
             pltpu.VMEM((HEADS * ROWS, KVL), f32),

time: 79.3 us -> 76.9 us (0.970); the launches traced: 79.1 us -> 75.7 us
  Pallas kernels: 77.5 us -> 74.1 us
    pallas_call x1, Pallas kernels: 77.5 us -> 74.1 us  [shards(): pl.pallas_call(kernel, out_shape=jax.ShapeDtypeStruct((ROWS, HEADS * VD),...]
where the time goes in v3:
time: 76.9 us; the launch traced here: 75.7 us
  Pallas kernels  74.1 us (96%)
  local copies, waits for them, and re-layouts  1.62 us (2%)
    pallas_call x1, Pallas kernels, shards(): pl.pallas_call(kernel, out_shape=jax.ShapeDtypeStruct((ROWS, HEADS * VD),...  74.1 us
    unnamed x1, local copies, waits for them, and re-layouts  1.62 us

profile of v3, /device:TPU:7, one launch (start us, length us, event | category | flops | bytes accessed | tf_op | source)
XLA Modules:
  0.0 75.7 jit_solution(1567456086586570603)
XLA Ops:
  0.0 74.1 %shard_map.82 = bf16[128,768]{1,0:T(8,128)(2,1)} custom-call(bf16[128,896]{1,0:T(8,128)(2,1)} %hid_hbm.1, bf16[576,896]{1,0:T(8,128)(2,1)} %bitcast.4, f32[1,512]{1,0:T(1,128)} %bitcast.5, bf16[512,768]{1,0:T(8,128)(2,1)} %wuk_hbm.1, bf16[512,768]{1,0:T(8,128)(2,1)} %wuv_hbm.1, bf16[128,1152]{1,0:T(8,128)(2,1)} %q_hbm.1, s32[1,128]{1,0:T(1,128)} %bitcast.6, ...), custom_call_target="tpu_custom_call" | custom-call | tf_op jit(solution)/shard_map/pallas_call | solution.py:384
  74.1 1.6 %copy.10 = bf16[128,768]{1,0:T(8,128)(2,1)} copy(bf16[128,768]{1,0:T(8,128)(2,1)} %shard_map.82) | data formatting | bytes 393216

commit v4 on v3

--- a/solution.py
+++ b/solution.py
@@ -187,6 +187,8 @@
     def route(kind, m):
         if (kind, m) == (0, 3):
             return 1, 2, block[2](m)
+        if (kind, m) == (1, 3):
+            return 2, 0, block[0](m)
         return first_axis[kind], second_axis[kind], block[kind](m)
 
     def phase1(kind, m):
@@ -311,47 +313,59 @@
     wait_recv(ag)
     each(one, 0, 1, 2, 3)
     each(two, 0, 1, 2, 3)
-    each(three, 0, 1, 2, 3)
-
-    wait_recv(share(0, 0, 0))
-    unit_x(0, (x + 0) % 4)
-    wait_recv(share(1, 1, 0))
-    unit_y(1, (y + 0) % 4)
-    wait_recv(share(2, 2, 0))
-    unit_z(2, (zl + 0) % 4)
-    each(five, 0, 1, 2)
-    each(four, 3)
-    wait_recv(share(0, 3, 0))
-    unit_3(0)
-    each(six, 0, 1, 2)
-    wait_recv(share(0, 0, 1))
-    unit_x(0, (x + 1) % 4)
-    wait_recv(share(1, 1, 1))
-    unit_y(1, (y + 1) % 4)
-    wait_recv(share(2, 2, 1))
-    unit_z(2, (zl + 1) % 4)
-    each(five, 3)
-    wait_recv(share(0, 0, 3))
-    unit_x(0, (x + 3) % 4)
-    each(seven, 0, 1, 2)
-    wait_recv(share(1, 1, 3))
-    unit_y(1, (y + 3) % 4)
-    each(six, 3)
-    wait_recv(share(2, 2, 3))
-    unit_z(2, (zl + 3) % 4)
-    wait_recv(share(0, 0, 2))
-    unit_x(0, (x + 2) % 4)
-    wait_recv(share(1, 1, 2))
-    unit_y(1, (y + 2) % 4)
-    each(seven, 3)
-    wait_recv(share(2, 2, 2))
-    unit_z(2, (zl + 2) % 4)
-    wait_recv(share(0, 3, 1))
-    unit_3(1)
-    wait_recv(share(0, 3, 3))
-    unit_3(3)
-    wait_recv(share(0, 3, 2))
-    unit_3(2)
+    each(three, 0, 1, 2)
+
+    def step(t, carry):
+        d = jnp.where(t < 2, t, 5 - t)
+        wait_recv(share(0, 0, d))
+        unit_x(0, (x + d) % 4)
+
+        @pl.when(t == 0)
+        def _():
+            each(three, 3)
+
+        @pl.when(t == 2)
+        def _():
+            each(seven, 0, 1, 2)
+
+        wait_recv(share(1, 1, d))
+        unit_y(1, (y + d) % 4)
+
+        @pl.when(t == 2)
+        def _():
+            each(six, 3)
+
+        @pl.when(t == 3)
+        def _():
+            each(seven, 3)
+
+        wait_recv(share(2, 2, d))
+        unit_z(2, (zl + d) % 4)
+
+        @pl.when(t == 0)
+        def _():
+            each(five, 0, 1, 2)
+            each(four, 3)
+
+        @pl.when(t == 1)
+        def _():
+            each(five, 3)
+
+        def last(i, carry):
+            d = jnp.where(t == 0, 0, jnp.where(i < 1, 1, 4 - i))
+            wait_recv(share(0, 3, d))
+            unit_3(d)
+            return carry
+
+        lax.fori_loop(0, jnp.where(t == 0, 1, jnp.where(t == 3, 3, 0)), last, 0)
+
+        @pl.when(t == 0)
+        def _():
+            each(six, 0, 1, 2)
+
+        return carry
+
+    lax.fori_loop(0, 4, step, 0)
 
     loads[3].wait()
     inverse = 1.0 / jnp.sum(l_s[...], axis=1, keepdims=True)

time: 76.9 us -> 76.3 us (level); the launches traced: 75.7 us -> 76.2 us
  no operation moved by 1% of the time
where the time goes in v4:
time: 76.3 us; the launch traced here: 76.2 us
  Pallas kernels  74.5 us (98%)
  local copies, waits for them, and re-layouts  1.62 us (2%)
    pallas_call x1, Pallas kernels, shards(): pl.pallas_call(kernel, out_shape=jax.ShapeDtypeStruct((ROWS, HEADS * VD),...  74.5 us
    unnamed x1, local copies, waits for them, and re-layouts  1.62 us

profile of v4, /device:TPU:7, one launch (start us, length us, event | category | flops | bytes accessed | tf_op | source)
XLA Modules:
  0.0 76.2 jit_solution(15807040013413695453)
XLA Ops:
  0.0 74.5 %shard_map.82 = bf16[128,768]{1,0:T(8,128)(2,1)} custom-call(bf16[128,896]{1,0:T(8,128)(2,1)} %hid_hbm.1, bf16[576,896]{1,0:T(8,128)(2,1)} %bitcast.4, f32[1,512]{1,0:T(1,128)} %bitcast.5, bf16[512,768]{1,0:T(8,128)(2,1)} %wuk_hbm.1, bf16[512,768]{1,0:T(8,128)(2,1)} %wuv_hbm.1, bf16[128,1152]{1,0:T(8,128)(2,1)} %q_hbm.1, s32[1,128]{1,0:T(1,128)} %bitcast.6, ...), custom_call_target="tpu_custom_call" | custom-call | tf_op jit(solution)/shard_map/pallas_call | solution.py:398
  74.5 1.6 %copy.10 = bf16[128,768]{1,0:T(8,128)(2,1)} copy(bf16[128,768]{1,0:T(8,128)(2,1)} %shard_map.82) | data formatting | bytes 393216
